TPU v7x, 256 devices: a whole 4x4x8 slice. The times are simulated.
256 devices in a mesh: pt: 16 (over y, x_lo, core), anc: 2 (over x_hi), head: 8 (over z).
Axes of the slice: x: 4 (x_hi: 2, x_lo: 2; x = x_hi * 2 + x_lo), y: 4, z: 8, core: 2. Of those that a mesh axis runs over, the one named last changes fastest.
Arguments:
- points: bfloat16 [8192, 1024], P(('pt', 'anc'), 'head'), may hold values from -6 to 6
- anchor_index: int32 [8192], replicated, may hold values from 0 to 8191
- tile_branch: int32 [32], P(('pt', 'anc')), may hold values 0 or 1
- norm_gain: float32 [1024], replicated, may hold values from 0.5 to 2
- q_surface: bfloat16 [1024, 1024], P(None, 'head'), as said below
- q_volume: bfloat16 [1024, 1024], P(None, 'head'), as said below
- kv_weight: bfloat16 [2, 1024, 1024], P(None, None, 'head'), may hold values from -0.1875 to 0.1875
- out_weight: bfloat16 [1024, 1024], P('head'), may hold values from -1.5 to 1.5
Outputs:
- point_update: bfloat16 [8192, 1024], P(('pt', 'anc'), 'head')
- anchor_update: bfloat16 [8192, 1024], P(('pt', 'anc'), 'head')
Inputs may be any that keep to these rules, and one draw needn't show every extreme that they name: `anchor_index`: every anchor names one query point; two anchors may name the same one. `q_surface`: entries of mean zero. `q_volume`: entries of mean zero.
All inputs are finite; a program needn't handle non-finite values. No bound on the sum of `tile_branch` on one device may be relied on, other than what follows from the above.
Results may differ from a plain program's by a relative error of at most 0.02.
The roundings to bfloat16 on the way count: a program that leaves them out, or rounds other values in their place, can miss the bound.
Values may be sent and summed in bfloat16 or wider, within the bound.
A program may use at most 64 MiB of HBM per device.

v0:
```python
import math

import jax
import jax.numpy as jnp
from jax import lax
from jax.sharding import PartitionSpec as P

HEAD_DIM = 64
TILE = 256


def absorb(state, query_block, key_block, value_block, open_all, volume_key):
    peak, total, acc = state
    scores = jnp.einsum("qhd,khd->hqk", query_block, key_block, preferred_element_type=jnp.float32)
    scores = scores / jnp.sqrt(jnp.float32(HEAD_DIM))
    visible = jnp.logical_or(open_all, volume_key)[None, None, :]
    scores = jnp.where(visible, scores, jnp.float32(-1e30))
    new_peak = jnp.maximum(peak, jnp.max(scores, axis=-1))
    factor = jnp.exp(peak - new_peak)
    weights = jnp.where(visible, jnp.exp(scores - new_peak[:, :, None]), jnp.float32(0.0))
    total = total * factor + jnp.sum(weights, axis=-1)
    rounded = weights.astype(jnp.bfloat16)
    acc = acc * jnp.transpose(factor)[:, :, None] + jnp.einsum(
        "hqk,khd->qhd", rounded, value_block, preferred_element_type=jnp.float32
    )
    return (new_peak, total, acc)


def attend_piece(carry, keys, values, queries, opens, half):
    heads_local = keys.shape[1] // HEAD_DIM
    count = keys.shape[0]
    block = math.gcd(count, 512)
    blocks = queries.shape[0] // TILE

    def one_step(step, state):
        first = step * block
        key_block = lax.dynamic_slice_in_dim(keys, step * block, block, 0).reshape(
            block, heads_local, HEAD_DIM
        )
        value_block = lax.dynamic_slice_in_dim(values, step * block, block, 0).reshape(
            block, heads_local, HEAD_DIM
        )
        volume_key = first + jnp.arange(block) >= half
        peak, total, acc = state
        peaks, totals, accs = ([], [], [])
        for index in range(blocks):
            low = index * TILE
            part_state = (
                peak[:, low : low + TILE],
                total[:, low : low + TILE],
                acc[low : low + TILE],
            )
            query_block = queries[low : low + TILE]
            open_all = opens[index]
            part_state = absorb(
                part_state, query_block, key_block, value_block, open_all, volume_key
            )
            peaks.append(part_state[0])
            totals.append(part_state[1])
            accs.append(part_state[2])
        return (
            jnp.concatenate(peaks, axis=1),
            jnp.concatenate(totals, axis=1),
            jnp.concatenate(accs, axis=0),
        )

    return lax.fori_loop(0, count // block, one_step, carry)


def shards(
    points, anchor_index, tile_branch, norm_gain, q_surface, q_volume, kv_weight, out_weight
):
    rows = points.shape[0]
    width = points.shape[1]
    heads_local = width // HEAD_DIM
    total_anchors = anchor_index.shape[0]
    half = total_anchors // 2
    whole = lax.all_gather(points, "head", axis=1, tiled=True)
    values_in = whole.astype(jnp.float32)
    scale = lax.rsqrt(jnp.mean(values_in * values_in, axis=-1, keepdims=True) + 1e-06)
    normed = (values_in * scale * norm_gain[None, :]).astype(jnp.bfloat16)
    column = lax.axis_index("head") * width
    group = lax.axis_index(("pt", "anc"))
    own_columns = lax.dynamic_slice_in_dim(normed, column, width, 1)
    local = anchor_index - group * rows
    inside = jnp.logical_and(local >= 0, local < rows)
    picked = jnp.take(own_columns, jnp.clip(local, 0, rows - 1), axis=0)
    table = jnp.where(inside[:, None], picked.astype(jnp.float32), jnp.float32(0.0))
    anchor_columns = lax.psum_scatter(
        table.astype(jnp.bfloat16), ("pt", "anc"), scatter_dimension=0, tiled=True
    )
    anchors = lax.all_gather(anchor_columns, "head", axis=1, tiled=True)
    anchor_count = anchors.shape[0]
    row_surface = jnp.repeat(tile_branch, TILE) == 1
    point_queries = jnp.where(
        row_surface[:, None],
        jnp.dot(normed, q_surface, preferred_element_type=jnp.float32),
        jnp.dot(normed, q_volume, preferred_element_type=jnp.float32),
    ).astype(jnp.bfloat16)
    anchor_surface = group * anchor_count + jnp.arange(anchor_count) < half
    anchor_queries = jnp.where(
        anchor_surface[:, None],
        jnp.dot(anchors, q_surface, preferred_element_type=jnp.float32),
        jnp.dot(anchors, q_volume, preferred_element_type=jnp.float32),
    ).astype(jnp.bfloat16)
    queries = jnp.concatenate([point_queries, anchor_queries], axis=0)
    all_rows = queries.shape[0]
    queries = queries.reshape(all_rows, heads_local, HEAD_DIM)
    opens = jnp.concatenate(
        [tile_branch == 1, jnp.ones((anchor_count // TILE,), jnp.bool_)], axis=0
    )
    start_state = (
        jnp.full((heads_local, all_rows), -1e30, jnp.float32),
        jnp.zeros((heads_local, all_rows), jnp.float32),
        jnp.zeros((all_rows, heads_local, HEAD_DIM), jnp.float32),
    )
    piece = lax.all_gather(anchors, ("pt", "anc"), axis=0, tiled=True)
    piece_keys = jnp.dot(piece, kv_weight[0], preferred_element_type=jnp.float32).astype(
        jnp.bfloat16
    )
    piece_values = jnp.dot(piece, kv_weight[1], preferred_element_type=jnp.float32).astype(
        jnp.bfloat16
    )
    peak, total, acc = attend_piece(start_state, piece_keys, piece_values, queries, opens, half)
    mixed = (acc / jnp.transpose(total)[:, :, None]).reshape(all_rows, width).astype(jnp.bfloat16)
    terms = jnp.dot(mixed, out_weight, preferred_element_type=jnp.float32)
    point_sum, anchor_sum = (
        lax.psum_scatter(
            terms[:rows].astype(jnp.bfloat16), "head", scatter_dimension=1, tiled=True
        ).astype(jnp.float32),
        lax.psum_scatter(
            terms[rows:].astype(jnp.bfloat16), "head", scatter_dimension=1, tiled=True
        ).astype(jnp.float32),
    )
    return (point_sum.astype(jnp.bfloat16), anchor_sum.astype(jnp.bfloat16))


def solution(mesh):
    in_specs = (
        P(("pt", "anc"), "head"),
        P(),
        P(("pt", "anc")),
        P(),
        P(None, "head"),
        P(None, "head"),
        P(None, None, "head"),
        P("head", None),
    )
    out_specs = (P(("pt", "anc"), "head"), P(("pt", "anc"), "head"))
    return jax.shard_map(shards, mesh=mesh, in_specs=in_specs, out_specs=out_specs, check_vma=False)
```

profile of v0, /device:TPU:8, one launch (start us, length us, event | category | flops | bytes accessed | tf_op | source)
XLA Modules:
  0.0 486.6 jit_solution(578075752857827109)
XLA Ops:
  7.2 0.8 fusion.30
  8.0 0.8 compare_and_fusion.1
  8.8 27.8 %all_gather.9 = bf16[256,1024]{1,0:T(8,128)(2,1)S(1)} all-gather(bf16[256,128]{1,0:T(8,128)(2,1)} %param.10), channel_id=1, replica_groups=mesh['pt'=16,'anc'=2,'head'=8] {'head'}, dimensions={1}, use_global_device_ids=true | all-gather | bytes 589824 | tf_op jit(solution)/shard_map/all_gather | solution.py:78
  36.8 0.9 fusion.25
  37.8 24.0 %gather_fusion = bf16[8192,128]{1,0:T(8,128)(2,1)S(1)} fusion(bf16[256,128]{1,0:T(8,128)(2,1)S(1)} %constant_dynamic-slice_fusion.2, s32[8192]{0:T(1024)S(1)} %fusion.30), kind=kCustom, calls=%fused_computation | custom fusion | bytes 4227072 | tf_op jit(solution)/shard_map/jit(_take)/gather | solution.py:87
  61.8 6.7 %select_convert_fusion = bf16[8192,128]{1,0:T(8,128)(2,1)} fusion(bf16[8192,128]{1,0:T(8,128)(2,1)S(1)} %gather_fusion, pred[8192]{0:T(1024)(128)(4,1)S(1)} %get-tuple-element.201, pred[8192]{0:T(1024)(128)(4,1)S(1)} %get-tuple-element.200), kind=kLoop, calls=%fused_computation.40 | loop fusion | flops 4194304 | bytes 4210688 | tf_op jit(solution)/shard_map/convert_element_type | solution.py:90
  68.6 129.5 %reduce-scatter.8.cloned.1.call-done = bf16[256,128]{1,0:T(8,128)(2,1)} async-done(((bf16[8192,128]{1,0:T(8,128)(2,1)}), bf16[256,128]{1,0:T(8,128)(2,1)}) %reduce-scatter.8.cloned.1.call-update) | async-done | bytes 65552 | tf_op jit(solution)/shard_map/reduce_scatter | solution.py:89
  198.1 27.8 %all_gather.10 = bf16[256,1024]{1,0:T(8,128)(2,1)} all-gather(bf16[256,128]{1,0:T(8,128)(2,1)} %reduce-scatter.8.cloned.1.call-done), channel_id=1, replica_groups=mesh['pt'=16,'anc'=2,'head'=8] {'head'}, dimensions={1}, use_global_device_ids=true | all-gather | bytes 589824 | tf_op jit(solution)/shard_map/all_gather | solution.py:92
  228.0 105.5 %all-gather.2.cloned.1.call-done = bf16[8192,1024]{1,0:T(8,128)(2,1)} async-done(((bf16[256,1024]{1,0:T(8,128)(2,1)}), bf16[8192,1024]{1,0:T(8,128)(2,1)}) %all-gather.2.cloned.1.call-update) | async-done | bytes 16777232 | tf_op jit(solution)/shard_map/all_gather | solution.py:117
  333.5 9.8 %convolution_convert_fusion = bf16[8192,128]{1,0:T(8,128)(2,1)} fusion(bf16[8192,1024]{1,0:T(8,128)(2,1)} %all-gather.2.cloned.1.call-done, bf16[2,1024,128]{2,1,0:T(8,128)(2,1)S(1)} %copy-done.5), kind=kOutput, calls=%fused_computation.38 | convolution fusion | flops 2148532224 | bytes 19136512 | tf_op jit(solution)/shard_map/dot_general | solution.py:121
  343.3 1.5 copy-done.4
  344.8 5.7 %convolution_convert_fusion.1 = bf16[8192,128]{1,0:T(8,128)(2,1)} fusion(bf16[8192,1024]{1,0:T(8,128)(2,1)S(1)} %copy-done.4, bf16[2,1024,128]{2,1,0:T(8,128)(2,1)S(1)} %copy-done.5), kind=kOutput, calls=%fused_computation.39 | convolution fusion | flops 2148532224 | bytes 19136512 | tf_op jit(solution)/shard_map/dot_general | solution.py:118
  350.6 49.6 %while.17 = (s32[]{:T(128)}, f32[2,512]{1,0:T(2,128)S(1)}, f32[2,512]{1,0:T(2,128)S(1)}, f32[512,2,64]{0,2,1:T(8,128)S(1)}, pred[1]{0:T(512)(128)(4,1)}, /*index...) while((s32[]{:T(128)}, f32[2,512]{1,0:T(2,128)S(1)}, ...), condition=%wide.region_7.8_spmd, body=%wide.region_2.0_spmd.sunk | while | flops 138353152 | bytes 9119916 | solution.py:67
  350.6 1.0 constant_dynamic-slice_fusion.4
  351.8 0.4 fusion.73
  352.1 0.4 fusion.74
  353.7 1.0 constant_dynamic-slice_fusion.4
  354.8 0.4 fusion.73
  355.2 0.4 fusion.74
  356.8 1.0 constant_dynamic-slice_fusion.4
  357.9 0.4 fusion.73
  358.3 0.4 fusion.74
  359.9 1.0 constant_dynamic-slice_fusion.4
  361.0 0.4 fusion.73
  361.4 0.4 fusion.74
  363.0 1.0 constant_dynamic-slice_fusion.4
  364.1 0.4 fusion.73
  364.5 0.4 fusion.74
  366.1 1.0 constant_dynamic-slice_fusion.4
  367.2 0.4 fusion.73
  367.6 0.4 fusion.74
  369.2 1.0 constant_dynamic-slice_fusion.4
  370.3 0.4 fusion.73
  370.7 0.4 fusion.74
  372.3 1.0 constant_dynamic-slice_fusion.4
  373.4 0.4 fusion.73
  373.8 0.4 fusion.74
  375.4 1.0 constant_dynamic-slice_fusion.4
  376.5 0.4 fusion.73
  376.9 0.4 fusion.74
  378.5 1.0 constant_dynamic-slice_fusion.4
  379.6 0.4 fusion.73
  381.6 1.0 constant_dynamic-slice_fusion.4
  382.7 0.4 fusion.73
  383.1 0.4 fusion.74
  384.7 1.0 constant_dynamic-slice_fusion.4
  385.8 0.4 fusion.73
  387.8 1.0 constant_dynamic-slice_fusion.4
  388.9 0.4 fusion.73
  389.3 0.4 fusion.74
  390.9 1.0 constant_dynamic-slice_fusion.4
  392.0 0.4 fusion.73
  394.0 1.0 constant_dynamic-slice_fusion.4
  395.1 0.4 fusion.73
  395.5 0.4 fusion.74
  397.1 1.0 constant_dynamic-slice_fusion.4
  398.2 0.4 fusion.73
  400.2 0.4 convolution_convert_fusion.2
  400.8 1.0 copy.27
  401.8 1.0 copy.29
  402.9 37.4 %reduce-scatter.10.cloned.1.call-done = bf16[128,256]{1,0:T(8,128)(2,1)} async-done(((bf16[1024,256]{1,0:T(8,128)(2,1)}), bf16[128,256]{1,0:T(8,128)(2,1)}) %reduce-scatter.10.cloned.1.call-update) | async-done | bytes 65552
  440.2 1.6 copy.28
  441.8 36.7 %reduce-scatter.12.cloned.1.call-done = bf16[128,256]{1,0:T(8,128)(2,1)} async-done(((bf16[1024,256]{1,0:T(8,128)(2,1)}), bf16[128,256]{1,0:T(8,128)(2,1)}) %reduce-scatter.12.cloned.1.call-update) | async-done | bytes 65552
  478.5 1.6 copy.30
  (230 shorter events, 23.9 us)
Async XLA Ops:
  7.2 393.1 %copy-start = (bf16[128,1024]{1,0:T(8,128)(2,1)S(1)}, bf16[128,1024]{1,0:T(8,128)(2,1)}, u32[]{:S(2)}) copy-start(bf16[128,1024]{1,0:T(8,128)(2,1)} %param.17) | copy-start | bytes 786436
  7.2 190.9 %reduce-scatter.8.cloned.1.call-start = ((), (), s32[]{:S(2)}) async-start(), calls=%async_computation.3 | async-start | bytes 2162688 | tf_op jit(solution)/shard_map/reduce_scatter | solution.py:89
  68.5 158.2 %copy-start.3 = (bf16[1024,128]{1,0:T(8,128)(2,1)S(1)}, bf16[1024,128]{1,0:T(8,128)(2,1)}, u32[]{:S(2)}) copy-start(bf16[1024,128]{1,0:T(8,128)(2,1)} %param.14) | copy-start | bytes 786436
  68.5 158.5 %copy-start.2 = (bf16[1024,128]{1,0:T(8,128)(2,1)S(1)}, bf16[1024,128]{1,0:T(8,128)(2,1)}, u32[]{:S(2)}) copy-start(bf16[1024,128]{1,0:T(8,128)(2,1)} %param.15) | copy-start | bytes 786436
  68.5 265.0 %all-gather.2.cloned.1.call-start = ((), (), s32[]{:S(2)}) async-start(), calls=%async_computation.4 | async-start | bytes 17301504 | tf_op jit(solution)/shard_map/all_gather | solution.py:117
  225.9 1.4 copy-start.1
  225.9 107.6 %copy-start.5 = (bf16[2,1024,128]{2,1,0:T(8,128)(2,1)S(1)}, bf16[2,1024,128]{2,1,0:T(8,128)(2,1)}, u32[]{:S(2)}) copy-start(bf16[2,1024,128]{2,1,0:T(8,128)(2,1)} %param.16) | copy-start | bytes 1572868
  225.9 214.3 %reduce-scatter.10.cloned.1.call-start = ((), (), s32[]{:S(2)}) async-start(), calls=%async_computation.5 | async-start | bytes 589824
  333.5 11.3 %copy-start.4 = (bf16[8192,1024]{1,0:T(8,128)(2,1)S(1)}, bf16[8192,1024]{1,0:T(8,128)(2,1)}, u32[]{:S(2)}) copy-start(bf16[8192,1024]{1,0:T(8,128)(2,1)} %all-gather.2.cloned.1.call-done) | copy-start | bytes 50331652
  401.8 76.7 %reduce-scatter.12.cloned.1.call-start = ((), (), s32[]{:S(2)}) async-start(), calls=%async_computation.6 | async-start | bytes 589824
Sparse Core Ops, SparseCore 0:
  68.7 129.3 reduce-scatter.7
  226.0 107.4 all-gather.1
  401.9 38.2 reduce-scatter.9
  442.6 35.8 reduce-scatter.11
where the time goes:
time: 487 us
  waiting for transfers between devices  309 us (63%)
  blocking collectives  55.6 us (11%)
  local copies, waits for them, and re-layouts  50.4 us (10%)
  matrix products  38.6 us (8%)
  other arithmetic  16.5 us (3%)
  between operations  14.7 us (3%)
    reduce_scatter x1, waiting for transfers between devices, shards(): lax.psum_scatter(table.astype(jnp.bfloat16), ('pt', 'anc'), scatter_dimen...  129 us
    all_gather x1, waiting for transfers between devices, shards(): piece = lax.all_gather(anchors, ('pt', 'anc'), axis=0, tiled=True)  105 us
    unnamed x6, waiting for transfers between devices  74.1 us
    all_gather x1, blocking collectives, shards(): anchors = lax.all_gather(anchor_columns, 'head', axis=1, tiled=True)  27.8 us
    all_gather x1, blocking collectives, shards(): whole = lax.all_gather(points, 'head', axis=1, tiled=True)  27.8 us
    gather x1, local copies, waits for them, and re-layouts, shards(): picked = jnp.take(own_columns, jnp.clip(local, 0, rows - 1), axis=0)  24 us
    dynamic_slice x32, local copies, waits for them, and re-layouts, one_step(): lax.dynamic_slice_in_dim(values, step * block, block, 0)  17.7 us
    dot_general x32, matrix products, absorb(): jnp.einsum('qhd,khd->hqk', query_block, key_block, preferred_element_type...  11.6 us
  transfers between devices with their start and end apart: 4, of which 4 were waited for; matrix products, arithmetic and copies ran while one was open for 1% of the time, Pallas kernels for 0%

commit v1 on v0

v1 whole, which is shorter than its diff:
```python
import functools

import jax
import jax.numpy as jnp
from jax import lax
from jax.experimental import pallas as pl
from jax.experimental.pallas import tpu as pltpu
from jax.sharding import PartitionSpec as P

MESH = pl.DeviceIdType.MESH
F32 = jnp.float32
BF16 = jnp.bfloat16
NEG = -1e30
T = 256
W = 128
G = 32
NZ = 8
NX = 4
LANES = 128


def group_of(x, y, c):
    return y * 8 + lax.rem(x, 2) * 4 + c * 2 + x // 2


def device_of(x, y, c, z):
    return (y * 4 + lax.rem(x, 2) * 2 + c, x // 2, z)


def nt(a, b):
    return lax.dot_general(a, b, (((1,), (1,)), ((), ())), preferred_element_type=F32)


def dot(a, b):
    return jnp.dot(a, b, preferred_element_type=F32)


class Copies:
    def __init__(self, send, recv):
        self.send, self.recv, self.count, self.sent = send, recv, 0, []

    def new(self):
        self.count += 1
        return self.count - 1

    def start(self, k, src, dst, device):
        copy = pltpu.make_async_remote_copy(
            src_ref=src,
            dst_ref=dst,
            send_sem=self.send.at[k],
            recv_sem=self.recv.at[k],
            device_id=device,
            device_id_type=MESH,
        )
        copy.start()
        self.sent.append(copy)

    def wait(self, k, landed):
        pltpu.make_async_remote_copy(
            src_ref=landed,
            dst_ref=landed,
            send_sem=self.send.at[k],
            recv_sem=self.recv.at[k],
            device_id=self.home,
            device_id_type=MESH,
        ).wait_recv()

    def drain(self):
        for copy in self.sent:
            copy.wait_send()
        self.sent = []


N_COPIES = 120


def kernel(
    points, idx, branch, gain, wqs, wqv, wkv, wo,
    outp, outa,
    gp, nrm, vqs, vqv, vkv, vwo, wcols, kv, qsv, qa, qx, qstage, qz, bias, stat, acc, mixed, mg,
    wsem, send, recv,
):
    pt, anc, z = lax.axis_index("pt"), lax.axis_index("anc"), lax.axis_index("head")
    c = lax.rem(pt, 2)
    x = anc * 2 + lax.rem(pt // 2, 2)
    y = pt // 4
    me = group_of(x, y, c)
    cp = Copies(send, recv)
    cp.home = (pt, anc, z)

    def step(i, d, n):
        return lax.rem(i + d + n, n)

    peers = [device_of(x, y, c, step(z, d, NZ)) for d in range(1, NZ)]
    peers += [device_of(step(x, d, NX), y, c, z) for d in range(1, NX)]
    peers += [device_of(x, step(y, d, NX), c, z) for d in range(1, NX)]
    sibling = device_of(x, y, 1 - c, z)
    peers += [sibling]
    barrier = pltpu.get_barrier_semaphore()
    for peer in peers:
        pl.semaphore_signal(barrier, inc=1, device_id=peer, device_id_type=MESH)

    weights = [
        pltpu.make_async_copy(src, dst, wsem.at[i])
        for i, (src, dst) in enumerate(((wqs, vqs), (wqv, vqv), (wkv, vkv), (wo, vwo)))
    ]
    for copy in weights:
        copy.start()
    gp[z] = points[...]
    pl.semaphore_wait(barrier, len(peers))

    def z_up(d):
        return device_of(x, y, c, step(z, d, NZ))

    def z_gather(own, buf):
        ids = [cp.new() for _ in range(8)]
        low, high = pl.ds(0, T // 2), pl.ds(T // 2, T // 2)

        def begin():
            cp.start(ids[0], own, buf.at[z], z_up(1))
            cp.start(ids[1], own, buf.at[z], z_up(-1))

        def hop(n):
            left, right = step(z, -n, NZ), step(z, n, NZ)

            def run():
                cp.wait(ids[2 * n - 2], buf.at[left])
                if n < 3:
                    cp.start(ids[2 * n], buf.at[left], buf.at[left], z_up(1))
                else:
                    cp.start(ids[6], buf.at[left, low], buf.at[left, low], z_up(1))
                cp.wait(ids[2 * n - 1], buf.at[right])
                if n < 3:
                    cp.start(ids[2 * n + 1], buf.at[right], buf.at[right], z_up(-1))
                else:
                    cp.start(ids[7], buf.at[right, high], buf.at[right, high], z_up(-1))

            return run

        def end():
            far = step(z, 4, NZ)
            cp.wait(ids[6], buf.at[far, low])
            cp.wait(ids[7], buf.at[far, high])

        return [begin, hop(1), hop(2), hop(3), end]

    gather = z_gather(points, gp)
    gather[0]()

    def tally(first, count):
        total = jnp.zeros((64, LANES), F32)
        for i in range(count):
            row = idx[:, pl.ds((first + i) * 1024, 1024)]
            high = (row // 128 == lax.broadcasted_iota(jnp.int32, (64, 1024), 0)).astype(F32)
            low = (lax.rem(row, 128) == lax.broadcasted_iota(jnp.int32, (128, 1024), 0)).astype(F32)
            total = total + nt(high.astype(BF16), low.astype(BF16))
        return total

    surface = tally(0, 4)
    gather[1]()
    volume = tally(4, 4)
    gather[2]()
    everyone = surface + volume

    def log_count(n):
        return jnp.where(n > 0.0, jnp.log(jnp.maximum(n, 1.0)), NEG)

    open_all = branch[0] == 1
    bias[0] = log_count(jnp.where(open_all, everyone, volume))
    bias[1] = log_count(everyone)
    gather[3]()
    for copy in weights:
        copy.wait()
    gather[4]()

    total = jnp.zeros((T, LANES), F32)
    for i in range(NZ):
        part = gp[i].astype(F32)
        total = total + part * part
    scale = lax.rsqrt(jnp.sum(total, axis=-1, keepdims=True) * (1.0 / 1024.0) + 1e-06)
    for i in range(NZ):
        columns = pl.ds(i * W, W)
        nrm[:, columns] = (gp[i].astype(F32) * scale * gain[:, columns]).astype(BF16)
    qsv[0] = dot(nrm[...], vqs[...]).astype(BF16) * BF16(0.125)
    qsv[1] = dot(nrm[...], vqv[...]).astype(BF16) * BF16(0.125)

    mine = y // 2
    qa[c, y] = qsv[mine]
    q_ids = [cp.new() for _ in range(3)]
    for d in (1, 2, 3):
        there = step(y, d, NX)
        cp.start(q_ids[d - 1], qsv.at[there // 2], qa.at[c, y], device_of(x, there, c, z))

    kv[me, :, 0:W] = dot(nrm[...], vkv[0]).astype(BF16)
    kv[me, :, W : 2 * W] = dot(nrm[...], vkv[1]).astype(BF16)

    u, v = (1 - c) * x + c * y, (1 - c) * y + c * x

    def place(i, j):
        return (1 - c) * i + c * j, (1 - c) * j + c * i

    def block(du, dv):
        bx, by = place(step(u, du, NX), step(v, dv, NX))
        return group_of(bx, by, c)

    def sibling_block(du, dv):
        bx, by = place(step(u, dv, NX), step(v, du, NX))
        return group_of(bx, by, 1 - c)

    def toward(du, dv):
        bx, by = place(step(u, du, NX), step(v, dv, NX))
        return device_of(bx, by, c, z)

    low, high = pl.ds(0, T // 2), pl.ds(T // 2, T // 2)
    u_ids = [cp.new() for _ in range(4)]
    v_ids = [[cp.new() for _ in range(4)] for _ in range(4)]
    s_ids = [[cp.new() for _ in range(4)] for _ in range(4)]

    def share(du):
        g = block(du, 0)
        cp.start(v_ids[du][0], kv.at[g], kv.at[g], toward(0, 1))
        cp.start(v_ids[du][1], kv.at[g], kv.at[g], toward(0, -1))

    def across(du, dv):
        g = block(du, dv)
        cp.start(s_ids[du][dv], kv.at[g], kv.at[g], sibling)

    def from_sibling(du, dv):
        cp.wait(s_ids[du][dv], kv.at[sibling_block(du, dv)])

    def begin_kv():
        g = block(0, 0)
        cp.start(u_ids[0], kv.at[g], kv.at[g], toward(1, 0))
        cp.start(u_ids[1], kv.at[g], kv.at[g], toward(-1, 0))
        share(0)
        across(0, 0)

    def u_hop():
        g = block(3, 0)
        cp.wait(u_ids[0], kv.at[g])
        cp.start(u_ids[2], kv.at[g, low], kv.at[g, low], toward(1, 0))
        g = block(1, 0)
        cp.wait(u_ids[1], kv.at[g])
        cp.start(u_ids[3], kv.at[g, high], kv.at[g, high], toward(-1, 0))
        for du in (3, 1):
            share(du)
            across(du, 0)

    def u_end():
        g = block(2, 0)
        cp.wait(u_ids[2], kv.at[g, low])
        cp.wait(u_ids[3], kv.at[g, high])
        share(2)
        across(2, 0)

    def v_hop(du):
        g = block(du, 3)
        cp.wait(v_ids[du][0], kv.at[g])
        cp.start(v_ids[du][2], kv.at[g, low], kv.at[g, low], toward(0, 1))
        across(du, 3)
        g = block(du, 1)
        cp.wait(v_ids[du][1], kv.at[g])
        cp.start(v_ids[du][3], kv.at[g, high], kv.at[g, high], toward(0, -1))
        across(du, 1)

    def v_end(du):
        g = block(du, 2)
        cp.wait(v_ids[du][2], kv.at[g, low])
        cp.wait(v_ids[du][3], kv.at[g, high])
        across(du, 2)

    begin_kv()
    w_ids = [cp.new() for _ in range(7)]
    for d in range(1, NZ):
        to = step(z, d, NZ)
        cp.start(w_ids[d - 1], vwo.at[:, pl.ds(pl.multiple_of(to * W, W), W)], wcols.at[z], z_up(d))
    wcols[z] = vwo[:, pl.ds(pl.multiple_of(z * W, W), W)]

    u_hop()

    for d in (1, 2, 3):
        cp.wait(q_ids[d - 1], qa.at[c, step(y, -d, NX)])
    q_sib = cp.new()
    cp.start(q_sib, qa.at[c], qa.at[c], sibling)
    u_end()
    v_hop(0)
    cp.wait(q_sib, qa.at[1 - c])

    x_ids = [cp.new() for _ in range(3)]
    for d in (1, 2, 3, 0):
        there = step(x, d, NX)
        g = group_of(there, y, c)
        for half in range(2):
            named = idx[:, pl.ds(pl.multiple_of(g * T + half * LANES, LANES), LANES)]
            named = jnp.transpose(jnp.broadcast_to(named, (LANES, LANES)))
            named = jnp.concatenate([named, named], axis=1)
            found = jnp.zeros((LANES, W), F32)
            for core in range(2):
                for row in range(NX):
                    base = group_of(x, row, core) * T
                    here = named - base == lax.broadcasted_iota(jnp.int32, (LANES, T), 1)
                    found = found + dot(here.astype(F32).astype(BF16), qa[core, row])
            rows = pl.ds(half * LANES, LANES)
            if d:
                qstage[d - 1, rows] = found.astype(BF16)
            else:
                qx[x, rows] = found.astype(BF16)
        if d:
            cp.start(x_ids[d - 1], qstage.at[d - 1], qx.at[x], device_of(there, y, c, z))
    v_end(0)
    for du in (3, 1, 2):
        v_hop(du)
        v_end(du)
    for du in range(4):
        for dv in range(4):
            from_sibling(du, dv)
    for d in (1, 2, 3):
        cp.wait(x_ids[d - 1], qx.at[step(x, -d, NX)])

    lane = lax.broadcasted_iota(jnp.int32, (T, W), 1)

    def split_heads(t, rows):
        rows = rows.astype(F32)
        qz[t, 0] = jnp.where(lane < 64, rows, 0.0).astype(BF16)
        qz[t, 1] = jnp.where(lane < 64, 0.0, rows).astype(BF16)

    split_heads(0, jnp.where(open_all, qsv[0].astype(F32), qsv[1].astype(F32)))
    split_heads(1, sum(qx[i].astype(F32) for i in range(NX)))

    stat[...] = jnp.full(stat.shape, 2.0 * NEG, F32)
    acc[...] = jnp.zeros(acc.shape, F32)
    ones = jnp.ones((T, LANES), BF16)

    def absorb(t, h, blocks):
        scores = []
        for g in blocks:
            s = nt(qz[t, h], kv[g, :, 0:W])
            extra = jnp.concatenate([bias[t, pl.ds(2 * g, 1)], bias[t, pl.ds(2 * g + 1, 1)]], axis=1)
            scores.append(s + extra)
        top = functools.reduce(jnp.maximum, scores)
        top = jnp.max(top, axis=-1, keepdims=True)
        old = stat[t, h]
        new = jnp.maximum(old, jnp.broadcast_to(top, (T, LANES)))
        factor = jnp.exp(old - new)
        stat[t, h] = new
        wide = jnp.concatenate([new, new], axis=1)
        added = None
        for g, s in zip(blocks, scores):
            p = jnp.exp(s - wide).astype(BF16)
            term = dot(p, jnp.concatenate([kv[g, :, W : 2 * W], ones], axis=1))
            added = term if added is None else added + term
        acc[t, h] = acc[t, h] * jnp.concatenate([factor, factor], axis=1) + added

    def finish(t):
        parts = [acc[t, h, :, 0:W] / acc[t, h, :, W : 2 * W] for h in range(2)]
        mixed[t] = jnp.where(lane < 64, parts[0], parts[1]).astype(BF16)
        mg[t, z] = mixed[t]

    def project(t, out):
        rows = jnp.concatenate([mg[t, i] for i in range(NZ)], axis=1)
        out[...] = dot(rows, wcols[...].reshape(NZ * W, W)).astype(BF16)

    for t in range(2):
        def one(i, carry):
            for h in range(2):
                absorb(t, h, [2 * i, 2 * i + 1])
            return carry

        lax.fori_loop(0, G // 2, one, 0)
        finish(t)

    gathers = [z_gather(mixed.at[t], mg.at[t]) for t in range(2)]
    for parts in zip(*gathers):
        for part in parts:
            part()
    for d in range(1, NZ):
        cp.wait(w_ids[d - 1], wcols.at[step(z, -d, NZ)])
    project(0, outp)
    project(1, outa)
    cp.drain()


def shards(points, anchor_index, tile_branch, norm_gain, q_surface, q_volume, kv_weight, out_weight):
    vmem = pl.BlockSpec(memory_space=pltpu.VMEM)
    anywhere = pl.BlockSpec(memory_space=pl.ANY)
    smem = pl.BlockSpec(memory_space=pltpu.SMEM)
    return pl.pallas_call(
        kernel,
        out_shape=(
            jax.ShapeDtypeStruct((T, W), BF16),
            jax.ShapeDtypeStruct((T, W), BF16),
        ),
        in_specs=[vmem, vmem, smem, vmem, anywhere, anywhere, anywhere, anywhere],
        out_specs=(vmem, vmem),
        scratch_shapes=[
            pltpu.VMEM((NZ, T, W), BF16),
            pltpu.VMEM((T, NZ * W), BF16),
            pltpu.VMEM((NZ * W, W), BF16),
            pltpu.VMEM((NZ * W, W), BF16),
            pltpu.VMEM((2, NZ * W, W), BF16),
            pltpu.VMEM((W, NZ * W), BF16),
            pltpu.VMEM((NZ, W, W), BF16),
            pltpu.VMEM((G, T, 2 * W), BF16),
            pltpu.VMEM((2, T, W), BF16),
            pltpu.VMEM((2, NX, T, W), BF16),
            pltpu.VMEM((NX, T, W), BF16),
            pltpu.VMEM((3, T, W), BF16),
            pltpu.VMEM((2, 2, T, W), BF16),
            pltpu.VMEM((2, 64, LANES), F32),
            pltpu.VMEM((2, 2, T, LANES), F32),
            pltpu.VMEM((2, 2, T, 2 * W), F32),
            pltpu.VMEM((2, T, W), BF16),
            pltpu.VMEM((2, NZ, T, W), BF16),
            pltpu.SemaphoreType.DMA((4,)),
            pltpu.SemaphoreType.DMA((N_COPIES,)),
            pltpu.SemaphoreType.DMA((N_COPIES,)),
        ],
        compiler_params=pltpu.CompilerParams(
            collective_id=0, has_side_effects=True, vmem_limit_bytes=50 * 1024 * 1024
        ),
    )(
        points,
        anchor_index.reshape(1, -1),
        tile_branch,
        norm_gain.reshape(1, -1),
        q_surface,
        q_volume,
        kv_weight,
        out_weight,
    )


def solution(mesh):
    in_specs = (
        P(("pt", "anc"), "head"),
        P(),
        P(("pt", "anc")),
        P(),
        P(None, "head"),
        P(None, "head"),
        P(None, None, "head"),
        P("head", None),
    )
    out_specs = (P(("pt", "anc"), "head"), P(("pt", "anc"), "head"))
    return jax.shard_map(shards, mesh=mesh, in_specs=in_specs, out_specs=out_specs, check_vma=False)
```

time: 487 us -> 101 us (0.21)
  waiting for transfers between devices: 309 us -> 0 us
  Pallas kernels: 0 us -> 92.2 us
  blocking collectives: 55.6 us -> 0 us
  local copies, waits for them, and re-layouts: 50.4 us -> 6.77 us
  matrix products: 38.6 us -> 0 us
  other arithmetic: 16.5 us -> 0 us
  between operations: 14.7 us -> 1.31 us
    reduce_scatter x1 -> x0, waiting for transfers between devices: 129 us -> none  [shards(): lax.psum_scatter(table.astype(jnp.bfloat16), ('pt', 'anc'), scatter_dimen...]
    all_gather x1 -> x0, waiting for transfers between devices: 105 us -> none  [shards(): piece = lax.all_gather(anchors, ('pt', 'anc'), axis=0, tiled=True)]
    pallas_call x0 -> x1, Pallas kernels: none -> 92.2 us  [shards(): pl.pallas_call(kernel, out_shape=(jax.ShapeDtypeStruct((T, W), BF16), jax...]
    unnamed x6 -> x0, waiting for transfers between devices: 74.1 us -> none
    all_gather x2 -> x0, blocking collectives: 55.6 us -> none  [the longest x1 27.8 us: shards(): anchors = lax.all_gather(anchor_columns, 'head', axis=1, tiled=True)]
    dot_general x71 -> x0, matrix products: 38.6 us -> none  [the longest x32 11.6 us: absorb(): jnp.einsum('qhd,khd->hqk', query_block, key_block, preferred_element_type...]
    gather x1 -> x0, local copies, waits for them, and re-layouts: 24 us -> none  [shards(): picked = jnp.take(own_columns, jnp.clip(local, 0, rows - 1), axis=0)]
    dynamic_slice x49 -> x0, local copies, waits for them, and re-layouts: 19.5 us -> none  [the longest x32 17.7 us: one_step(): lax.dynamic_slice_in_dim(values, step * block, block, 0)]
  transfers between devices with their start and end apart: 4 -> 0, of which waited for: 4 -> 0; matrix products, arithmetic and copies ran while one was open for 1% -> 0% of each run, Pallas kernels for 0% -> 0%
where the time goes in v1:
time: 101 us; the launch traced here: 100 us
  Pallas kernels  92.2 us (91%)
  local copies, waits for them, and re-layouts  6.77 us (7%)
  between operations  1.31 us (1%)
    pallas_call x1, Pallas kernels, shards(): pl.pallas_call(kernel, out_shape=(jax.ShapeDtypeStruct((T, W), BF16), jax...  92.2 us
    unnamed x16, local copies, waits for them, and re-layouts  6.77 us

profile of v1, /device:TPU:8, one launch (start us, length us, event | category | flops | bytes accessed | tf_op | source)
XLA Modules:
  0.0 100.3 jit_solution(3491750294321238406)
XLA Ops:
  0.6 0.0 copy-start.6
  1.3 0.0 copy-done.6
  1.3 0.0 copy-start
  1.3 1.0 %copy-done = bf16[2,1024,128]{2,1,0:T(8,128)(2,1)S(1)} copy-done((bf16[2,1024,128]{2,1,0:T(8,128)(2,1)S(1)}, bf16[2,1024,128]{2,1,0:T(8,128)(2,1)}, u32[]{:S(2)}) %copy-start) | copy-done | bytes 524312
  2.4 0.0 copy-start.1
  2.4 0.9 copy-done.1
  3.3 0.0 copy-start.2
  3.3 0.9 copy-done.2
  4.3 0.0 copy-start.3
  4.3 0.9 copy-done.3
  5.2 0.0 copy-start.4
  5.2 0.8 copy-done.4
  6.1 0.0 copy-start.5
  6.1 0.8 copy-done.5
  6.8 92.2 %shard_map.95 = (bf16[256,128]{1,0:T(8,128)(2,1)S(1)}, bf16[256,128]{1,0:T(8,128)(2,1)S(1)}) custom-call(bf16[256,128]{1,0:T(8,128)(2,1)S(1)} %copy-done.4, s32[1,8192]{1,0:T(1,128)S(1)} %bitcast.2, s32[1]{0:T(128)S(6)} %copy.12.branch, f32[1,1024]{1,0:T(1,128)S(1)} %bitcast.3, bf16[1024,128]{1,0:T(8,128)(2,1)S(1)} %copy-done.1, ...), custom_call_target="tpu_custom_call" | custom-call | tf_op jit(solution)/shard_map/pallas_call | solution.py:387
  99.0 0.6 copy.13
  99.6 0.6 copy.14
Async XLA Ops:
  0.6 0.7 copy-start.6
  1.3 1.0 %copy-start = (bf16[2,1024,128]{2,1,0:T(8,128)(2,1)S(1)}, bf16[2,1024,128]{2,1,0:T(8,128)(2,1)}, u32[]{:S(2)}) copy-start(bf16[2,1024,128]{2,1,0:T(8,128)(2,1)} %wkv.1) | copy-start | bytes 1572868
  2.4 0.9 copy-start.1
  3.3 0.9 copy-start.2
  4.3 0.9 copy-start.3
  5.2 0.8 copy-start.4
  6.1 0.8 copy-start.5

commit v2 on v1

v2 whole, which is shorter than its diff:
```python
import jax
import jax.numpy as jnp
from jax import lax
from jax.experimental import pallas as pl
from jax.experimental.pallas import tpu as pltpu
from jax.sharding import PartitionSpec as P

MESH = pl.DeviceIdType.MESH
F32 = jnp.float32
BF16 = jnp.bfloat16
NEG = -1e30
T = 256
W = 128
G = 32
NZ = 8
NX = 4
LANES = 128
D = 1024
N_COPIES = 128
CHUNK = 4
ORDER = (
    (0, 0), (3, 0), (1, 0), (0, 3),
    (0, 1), (2, 0), (3, 3), (3, 1),
    (1, 3), (1, 1), (0, 2), (2, 3),
    (2, 1), (3, 2), (1, 2), (2, 2),
)
SLOT = {pair: i for i, pair in enumerate(ORDER)}


def group_of(x, y, c):
    return y * 8 + lax.rem(x, 2) * 4 + c * 2 + x // 2


def device_of(x, y, c, z):
    return (y * 4 + lax.rem(x, 2) * 2 + c, x // 2, z)


def nt(a, b):
    return lax.dot_general(a, b, (((1,), (1,)), ((), ())), preferred_element_type=F32)


def dot(a, b):
    return jnp.dot(a, b, preferred_element_type=F32)


class Copies:
    def __init__(self, send, recv, home):
        self.send, self.recv, self.home, self.count, self.sent = send, recv, home, 0, []

    def new(self):
        self.count += 1
        return self.count - 1

    def make(self, k, src, dst, device):
        return pltpu.make_async_remote_copy(
            src_ref=src,
            dst_ref=dst,
            send_sem=self.send.at[k],
            recv_sem=self.recv.at[k],
            device_id=device,
            device_id_type=MESH,
        )

    def start(self, k, src, dst, device):
        copy = self.make(k, src, dst, device)
        copy.start()
        self.sent.append(copy)

    def wait(self, k, landed):
        self.make(k, landed, landed, self.home).wait_recv()

    def drain(self):
        for copy in self.sent:
            copy.wait_send()


def kernel(
    points, idx_in, branch, gain_in, wqs, wqv, wkv, wo,
    outp, outa,
    idx, gain, gp, nrm, vqs, vqv, vkv, vwo, wcols, kv, ext, logs, qsv, qa, qx, qstage, qe,
    stat, acc, even, odd, mg,
    wsem, send, recv,
):
    pt, anc, z = lax.axis_index("pt"), lax.axis_index("anc"), lax.axis_index("head")
    c = lax.rem(pt, 2)
    x = anc * 2 + lax.rem(pt // 2, 2)
    y = pt // 4
    cp = Copies(send, recv, (pt, anc, z))

    def step(i, d, n):
        return lax.rem(i + d + n, n)

    peers = [device_of(x, y, c, step(z, d, NZ)) for d in range(1, NZ)]
    peers += [device_of(step(x, d, NX), y, c, z) for d in range(1, NX)]
    peers += [device_of(x, step(y, d, NX), c, z) for d in range(1, NX)]
    sibling = device_of(x, y, 1 - c, z)
    peers += [sibling]
    barrier = pltpu.get_barrier_semaphore()
    for peer in peers:
        pl.semaphore_signal(barrier, inc=1, device_id=peer, device_id_type=MESH)

    pairs = (
        (points, gp.at[z]), (idx_in, idx), (gain_in, gain),
        (wkv, vkv), (wqs, vqs), (wqv, vqv), (wo, vwo),
    )
    loads = [pltpu.make_async_copy(src, dst, wsem.at[i]) for i, (src, dst) in enumerate(pairs)]
    for load in loads:
        load.start()
    loads[0].wait()
    pl.semaphore_wait(barrier, len(peers))

    def z_up(d):
        return device_of(x, y, c, step(z, d, NZ))

    low, high = pl.ds(0, T // 2), pl.ds(T // 2, T // 2)

    def z_gather(buf):
        ids = [cp.new() for _ in range(8)]

        def begin():
            for k, d in enumerate((2, -2, 1, -1)):
                cp.start(ids[k], buf.at[z], buf.at[z], z_up(d))

        def forward():
            at = step(z, -2, NZ)
            cp.wait(ids[0], buf.at[at])
            cp.start(ids[4], buf.at[at], buf.at[at], z_up(1))
            cp.start(ids[6], buf.at[at, low], buf.at[at, low], z_up(2))
            at = step(z, 2, NZ)
            cp.wait(ids[1], buf.at[at])
            cp.start(ids[5], buf.at[at], buf.at[at], z_up(-1))
            cp.start(ids[7], buf.at[at, high], buf.at[at, high], z_up(-2))

        def end():
            for k, d in ((2, -1), (3, 1), (4, -3), (5, 3)):
                cp.wait(ids[k], buf.at[step(z, d, NZ)])
            at = step(z, 4, NZ)
            cp.wait(ids[6], buf.at[at, low])
            cp.wait(ids[7], buf.at[at, high])

        return begin, forward, end

    begin, forward, end = z_gather(gp)
    begin()

    def tally(first, count):
        total = jnp.zeros((64, LANES), F32)
        for i in range(count):
            row = idx[:, pl.ds((first + i) * 1024, 1024)]
            upper = (row // 128 == lax.broadcasted_iota(jnp.int32, (64, 1024), 0)).astype(F32)
            lower = (lax.rem(row, 128) == lax.broadcasted_iota(jnp.int32, (128, 1024), 0)).astype(F32)
            total = total + nt(upper.astype(BF16), lower.astype(BF16))
        return total

    loads[1].wait()
    surface = tally(0, 4)
    volume = tally(4, 4)
    everyone = surface + volume
    open_all = branch[0] == 1

    def log_count(n):
        return jnp.where(n > 0.0, jnp.log(jnp.maximum(n, 1.0)), NEG)

    for t, n in enumerate((jnp.where(open_all, everyone, volume), everyone)):
        rest = log_count(n)
        for j in range(3):
            term = rest.astype(BF16).astype(F32)
            logs[3 * t + j] = term
            rest = rest - term
    forward()

    u, v = (1 - c) * x + c * y, (1 - c) * y + c * x

    def place(i, j):
        return (1 - c) * i + c * j, (1 - c) * j + c * i

    def group_at(slot):
        du, dv = ORDER[slot % 16]
        if slot < 16:
            bx, by = place(step(u, du, NX), step(v, dv, NX))
            return group_of(bx, by, c)
        bx, by = place(step(u, dv, NX), step(v, du, NX))
        return group_of(bx, by, 1 - c)

    sub = lax.broadcasted_iota(jnp.int32, (8, LANES), 0)
    for slot in range(G):
        g = group_at(slot)
        for half in range(2):
            terms = jnp.zeros((8, LANES), F32)
            for j in range(6):
                terms = jnp.where(sub == j, logs[j, pl.ds(2 * g + half, 1)], terms)
            terms = jnp.concatenate([terms, jnp.zeros((LANES - 8, LANES), F32)], axis=0)
            ext[slot, pl.ds(half * LANES, LANES)] = jnp.transpose(terms).astype(BF16)

    for load in loads[2:]:
        load.wait()
    end()

    total = jnp.zeros((T, LANES), F32)
    for i in range(NZ):
        part = gp[i].astype(F32)
        total = total + part * part
    scale = lax.rsqrt(jnp.sum(total, axis=-1, keepdims=True) * (1.0 / D) + 1e-06)
    for i in range(NZ):
        columns = pl.ds(i * W, W)
        nrm[:, columns] = (gp[i].astype(F32) * scale * gain[:, columns]).astype(BF16)
    keys = dot(nrm[...], vkv[0]).astype(BF16)
    kv[0, W : 2 * W, 0:LANES] = keys[:LANES]
    kv[0, W : 2 * W, LANES : 2 * LANES] = keys[LANES:]
    kv[0, 0:W] = jnp.transpose(dot(nrm[...], vkv[1])).astype(BF16)
    qsv[0] = dot(nrm[...], vqs[...]).astype(BF16) * BF16(0.125)
    qsv[1] = dot(nrm[...], vqv[...]).astype(BF16) * BF16(0.125)

    def toward(du, dv):
        bx, by = place(step(u, du, NX), step(v, dv, NX))
        return device_of(bx, by, c, z)

    u_ids = [cp.new() for _ in range(4)]
    v_ids = [[cp.new() for _ in range(4)] for _ in range(4)]
    s_ids = [cp.new() for _ in range(16)]

    def pass_on(k, src, dst, device, rows=None):
        src, dst = SLOT[src], SLOT[dst]
        if rows is None:
            cp.start(k, kv.at[src], kv.at[dst], device)
        else:
            cp.start(k, kv.at[src, rows], kv.at[dst, rows], device)

    def landed(k, pair, rows=None):
        slot = SLOT[pair]
        cp.wait(k, kv.at[slot] if rows is None else kv.at[slot, rows])

    def share(du):
        pass_on(v_ids[du][0], (du, 0), (du, 3), toward(0, 1))
        pass_on(v_ids[du][1], (du, 0), (du, 1), toward(0, -1))

    def across(pair):
        slot = SLOT[pair]
        cp.start(s_ids[slot], kv.at[slot], kv.at[16 + slot], sibling)

    def from_sibling(first, count):
        for slot in range(first, first + count):
            cp.wait(s_ids[slot], kv.at[16 + slot])

    def u_hop():
        landed(u_ids[0], (3, 0))
        pass_on(u_ids[2], (3, 0), (2, 0), toward(1, 0), low)
        share(3)
        landed(u_ids[1], (1, 0))
        pass_on(u_ids[3], (1, 0), (2, 0), toward(-1, 0), high)
        share(1)
        across((3, 0))
        across((1, 0))

    def u_end():
        landed(u_ids[2], (2, 0), low)
        landed(u_ids[3], (2, 0), high)
        share(2)
        across((2, 0))

    def v_hop(du):
        landed(v_ids[du][0], (du, 3))
        pass_on(v_ids[du][2], (du, 3), (du, 2), toward(0, 1), low)
        landed(v_ids[du][1], (du, 1))
        pass_on(v_ids[du][3], (du, 1), (du, 2), toward(0, -1), high)
        across((du, 3))
        across((du, 1))

    def v_end(du):
        landed(v_ids[du][2], (du, 2), low)
        landed(v_ids[du][3], (du, 2), high)
        across((du, 2))

    pass_on(u_ids[0], (0, 0), (3, 0), toward(1, 0))
    pass_on(u_ids[1], (0, 0), (1, 0), toward(-1, 0))
    share(0)

    mine = y // 2
    q_ids = [cp.new() for _ in range(4)]
    for d in (1, 2, 3):
        there = step(y, d, NX)
        cp.start(q_ids[d], qsv.at[there // 2], qa.at[c, y], device_of(x, there, c, z))
    qa[c, y] = qsv[mine]
    across((0, 0))

    w_ids = [cp.new() for _ in range(NZ)]
    for d in range(1, NZ):
        to = pl.multiple_of(step(z, d, NZ) * W, W)
        cp.start(w_ids[d], vwo.at[:, pl.ds(to, W)], wcols.at[z], z_up(d))
    wcols[z] = vwo[:, pl.ds(pl.multiple_of(z * W, W), W)]

    lane = lax.broadcasted_iota(jnp.int32, (T, W), 1)

    def split_heads(t, rows):
        marks = jnp.where(lane // 3 == t, 1.0, 0.0).astype(BF16)
        for h in range(2):
            qe[t, h, :, 0:W] = jnp.where(lane // 64 == h, rows, 0.0).astype(BF16)
            qe[t, h, :, W : 2 * W] = marks

    split_heads(0, jnp.where(open_all, qsv[0].astype(F32), qsv[1].astype(F32)))
    stat[...] = jnp.full(stat.shape, 2.0 * NEG, F32)
    acc[...] = jnp.zeros(acc.shape, F32)
    ones = jnp.ones((16, T), BF16)

    def fill(t, h, first, buf):
        top = None
        for j in range(CHUNK):
            slot = first + j
            k = jnp.concatenate([kv[slot, W : 2 * W, 0:LANES], kv[slot, W : 2 * W, LANES : 2 * LANES]], axis=0)
            s = nt(jnp.concatenate([k, ext[slot]], axis=1), qe[t, h])
            buf[j] = s
            top = s if top is None else jnp.maximum(top, s)
        return jnp.max(top, axis=0, keepdims=True)

    def absorb(t, h, first, buf, top):
        old = stat[t, h, 0:1]
        new = jnp.maximum(old, top)
        factor = jnp.exp(old - new)
        stat[t, h, 0:1] = new
        added = None
        for j in range(CHUNK):
            p = jnp.exp(buf[j] - new).astype(BF16)
            values = jnp.concatenate([kv[first + j, pl.ds(h * 64, 64)], ones], axis=0)
            term = dot(values, p)
            added = term if added is None else added + term
        acc[t, h] = acc[t, h] * factor + added

    def attend(t, first, chunks):
        last = first + (chunks - 1) * CHUNK
        top = fill(t, 0, first, even)

        def one(i, top):
            at = first + i * CHUNK
            other = fill(t, 1, at, odd)
            absorb(t, 0, at, even, top)
            top = fill(t, 0, jnp.minimum(at + CHUNK, last), even)
            absorb(t, 1, at, odd, other)
            return top

        if chunks > 1:
            top = lax.fori_loop(0, chunks - 1, one, top)
        other = fill(t, 1, last, odd)
        absorb(t, 0, last, even, top)
        absorb(t, 1, last, odd, other)

    def finish(t):
        parts = [acc[t, h, 0:64] / acc[t, h, 64:65] for h in range(2)]
        mg[t, z] = jnp.transpose(jnp.concatenate(parts, axis=0)).astype(BF16)

    def project(t, out):
        rows = jnp.concatenate([mg[t, i] for i in range(NZ)], axis=1)
        out[...] = dot(rows, wcols[...].reshape(NZ * W, W)).astype(BF16)

    x_ids = [cp.new() for _ in range(4)]

    def select():
        for d in (1, 2, 3, 0):
            there = step(x, d, NX)
            g = group_of(there, y, c)
            for half in range(2):
                named = idx[:, pl.ds(pl.multiple_of(g * T + half * LANES, LANES), LANES)]
                named = jnp.transpose(jnp.broadcast_to(named, (LANES, LANES)))
                named = jnp.concatenate([named, named], axis=1)
                found = jnp.zeros((LANES, W), F32)
                for core in range(2):
                    for row in range(NX):
                        base = group_of(x, row, core) * T
                        here = named - base == lax.broadcasted_iota(jnp.int32, (LANES, T), 1)
                        found = found + dot(here.astype(F32).astype(BF16), qa[core, row])
                rows = pl.ds(half * LANES, LANES)
                if d:
                    qstage[d - 1, rows] = found.astype(BF16)
                else:
                    qx[x, rows] = found.astype(BF16)
            if d:
                cp.start(x_ids[d], qstage.at[d - 1], qx.at[x], device_of(there, y, c, z))

    u_hop()
    for d in (1, 2, 3):
        cp.wait(q_ids[d], qa.at[c, step(y, -d, NX)])
    cp.start(q_ids[0], qa.at[c], qa.at[c], sibling)
    v_hop(0)
    attend(0, 0, 1)
    u_end()
    v_hop(3)
    v_hop(1)
    cp.wait(q_ids[0], qa.at[1 - c])
    select()
    v_end(0)
    v_hop(2)
    attend(0, 4, 2)
    v_end(3)
    v_end(1)
    from_sibling(0, 8)
    attend(0, 16, 2)
    v_end(2)
    attend(0, 12, 1)
    for d in (1, 2, 3):
        cp.wait(x_ids[d], qx.at[step(x, -d, NX)])
    split_heads(1, sum(qx[i].astype(F32) for i in range(NX)))
    attend(1, 0, 6)
    from_sibling(8, 8)
    attend(0, 24, 2)
    finish(0)
    point_steps = z_gather(mg.at[0])
    point_steps[0]()
    attend(1, 24, 2)
    point_steps[1]()
    finish(1)
    anchor_steps = z_gather(mg.at[1])
    anchor_steps[0]()
    for d in range(1, NZ):
        cp.wait(w_ids[d], wcols.at[step(z, -d, NZ)])
    point_steps[2]()
    anchor_steps[1]()
    project(0, outp)
    anchor_steps[2]()
    project(1, outa)
    cp.drain()


def shards(points, anchor_index, tile_branch, norm_gain, q_surface, q_volume, kv_weight, out_weight):
    vmem = pl.BlockSpec(memory_space=pltpu.VMEM)
    anywhere = pl.BlockSpec(memory_space=pl.ANY)
    smem = pl.BlockSpec(memory_space=pltpu.SMEM)
    return pl.pallas_call(
        kernel,
        out_shape=(
            jax.ShapeDtypeStruct((T, W), BF16),
            jax.ShapeDtypeStruct((T, W), BF16),
        ),
        in_specs=[anywhere, anywhere, smem, anywhere, anywhere, anywhere, anywhere, anywhere],
        out_specs=(vmem, vmem),
        scratch_shapes=[
            pltpu.VMEM((1, G * T), jnp.int32),
            pltpu.VMEM((1, D), F32),
            pltpu.VMEM((NZ, T, W), BF16),
            pltpu.VMEM((T, D), BF16),
            pltpu.VMEM((D, W), BF16),
            pltpu.VMEM((D, W), BF16),
            pltpu.VMEM((2, D, W), BF16),
            pltpu.VMEM((W, D), BF16),
            pltpu.VMEM((NZ, W, W), BF16),
            pltpu.VMEM((G, 2 * W, T), BF16),
            pltpu.VMEM((G, T, LANES), BF16),
            pltpu.VMEM((8, 64, LANES), F32),
            pltpu.VMEM((2, T, W), BF16),
            pltpu.VMEM((2, NX, T, W), BF16),
            pltpu.VMEM((NX, T, W), BF16),
            pltpu.VMEM((3, T, W), BF16),
            pltpu.VMEM((2, 2, T, 2 * W), BF16),
            pltpu.VMEM((2, 2, 8, T), F32),
            pltpu.VMEM((2, 2, 80, T), F32),
            pltpu.VMEM((CHUNK, T, T), F32),
            pltpu.VMEM((CHUNK, T, T), F32),
            pltpu.VMEM((2, NZ, T, W), BF16),
            pltpu.SemaphoreType.DMA((7,)),
            pltpu.SemaphoreType.DMA((N_COPIES,)),
            pltpu.SemaphoreType.DMA((N_COPIES,)),
        ],
        compiler_params=pltpu.CompilerParams(
            collective_id=0, has_side_effects=True, vmem_limit_bytes=60 * 1024 * 1024
        ),
    )(
        points,
        anchor_index.reshape(1, -1),
        tile_branch,
        norm_gain.reshape(1, -1),
        q_surface,
        q_volume,
        kv_weight,
        out_weight,
    )


def solution(mesh):
    in_specs = (
        P(("pt", "anc"), "head"),
        P(),
        P(("pt", "anc")),
        P(),
        P(None, "head"),
        P(None, "head"),
        P(None, None, "head"),
        P("head", None),
    )
    out_specs = (P(("pt", "anc"), "head"), P(("pt", "anc"), "head"))
    return jax.shard_map(shards, mesh=mesh, in_specs=in_specs, out_specs=out_specs, check_vma=False)
```

time: 101 us -> 70.1 us (0.69)
  Pallas kernels: 92.2 us -> 65.9 us
  local copies, waits for them, and re-layouts: 6.77 us -> 2.14 us
    pallas_call x1, Pallas kernels: 92.2 us -> 65.9 us  [shards(): pl.pallas_call(kernel, out_shape=(jax.ShapeDtypeStruct((T, W), BF16), jax...]
    unnamed x16 -> x4, local copies, waits for them, and re-layouts: 6.77 us -> 2.14 us
where the time goes in v2:
time: 70.1 us; the launch traced here: 69.3 us
  Pallas kernels  65.9 us (94%)
  local copies, waits for them, and re-layouts  2.14 us (3%)
  between operations  1.29 us (2%)
    pallas_call x1, Pallas kernels, shards(): pl.pallas_call(kernel, out_shape=(jax.ShapeDtypeStruct((T, W), BF16), jax...  65.9 us
    unnamed x4, local copies, waits for them, and re-layouts  2.14 us

profile of v2, /device:TPU:8, one launch (start us, length us, event | category | flops | bytes accessed | tf_op | source)
XLA Modules:
  0.0 69.3 jit_solution(7993882798339327563)
XLA Ops:
  1.3 65.9 %shard_map.95 = (bf16[256,128]{1,0:T(8,128)(2,1)}, bf16[256,128]{1,0:T(8,128)(2,1)}) custom-call(bf16[256,128]{1,0:T(8,128)(2,1)} %points.1, s32[1,8192]{1,0:T(1,128)} %bitcast.2, s32[1]{0:T(128)S(6)} %copy.12.branch, f32[1,1024]{1,0:T(1,128)} %bitcast.3, bf16[1024,128]{1,0:T(8,128)(2,1)} %wqs.1, bf16[1024,128]{1,0:T(8,128)(2,1)} %wqv.1, ...), custom_call_target="tpu_custom_call" | custom-call | tf_op jit(solution)/shard_map/pallas_call | solution.py:426
  67.2 0.0 copy-start
  67.2 1.5 %copy.13 = bf16[256,128]{1,0:T(8,128)(2,1)} copy(bf16[256,128]{1,0:T(8,128)(2,1)} %get-tuple-element.4) | data formatting | bytes 131072
  68.7 0.0 copy-done
  68.7 0.6 copy.14
Async XLA Ops:
  67.2 1.5 %copy-start = (bf16[256,128]{1,0:T(8,128)(2,1)S(1)}, bf16[256,128]{1,0:T(8,128)(2,1)}, u32[]{:S(2)}) copy-start(bf16[256,128]{1,0:T(8,128)(2,1)} %get-tuple-element.5) | copy-start | bytes 196612

commit v3 on v2

v3 whole, which is shorter than its diff:
```python
import jax
import jax.numpy as jnp
from jax import lax
from jax.experimental import pallas as pl
from jax.experimental.pallas import tpu as pltpu
from jax.sharding import PartitionSpec as P

MESH = pl.DeviceIdType.MESH
F32 = jnp.float32
BF16 = jnp.bfloat16
NEG = -1e30
T = 256
W = 128
G = 32
NZ = 8
NX = 4
LANES = 128
D = 1024
N_COPIES = 128
H = T // 2
PART = T // NZ
CHUNK = 4
ORDER = (
    (0, 0), (3, 0), (1, 0), (2, 0),
    (0, 3), (0, 1), (3, 3), (3, 1),
    (1, 3), (1, 1), (2, 3), (2, 1),
    (0, 2), (3, 2), (1, 2), (2, 2),
)
SLOT = {pair: i for i, pair in enumerate(ORDER)}


def group_of(x, y, c):
    return y * 8 + lax.rem(x, 2) * 4 + c * 2 + x // 2


def device_of(x, y, c, z):
    return (y * 4 + lax.rem(x, 2) * 2 + c, x // 2, z)


def nt(a, b):
    return lax.dot_general(a, b, (((1,), (1,)), ((), ())), preferred_element_type=F32)


def dot(a, b):
    return jnp.dot(a, b, preferred_element_type=F32)


class Copies:
    def __init__(self, send, recv, home):
        self.send, self.recv, self.home, self.count, self.sent = send, recv, home, 0, []

    def new(self):
        self.count += 1
        return self.count - 1

    def make(self, k, src, dst, device):
        return pltpu.make_async_remote_copy(
            src_ref=src,
            dst_ref=dst,
            send_sem=self.send.at[k],
            recv_sem=self.recv.at[k],
            device_id=device,
            device_id_type=MESH,
        )

    def start(self, k, src, dst, device):
        copy = self.make(k, src, dst, device)
        copy.start()
        self.sent.append(copy)

    def wait(self, k, landed):
        self.make(k, landed, landed, self.home).wait_recv()

    def drain(self, count):
        for copy in self.sent[:count]:
            copy.wait_send()
        self.sent = self.sent[count:]


def kernel(
    points, idx_in, branch, gain_in, wqs, wqv, wkv, wo,
    out,
    idx, gain, gp, nrm, vqs, vqv, vkv, wall, kv, ext, logs, qsv, qa, qx, qstage, qe,
    stat, acc, even, odd, mixed, rows_in, rows_out, done,
    wsem, send, recv,
):
    pt, anc, z = lax.axis_index("pt"), lax.axis_index("anc"), lax.axis_index("head")
    c = lax.rem(pt, 2)
    x = anc * 2 + lax.rem(pt // 2, 2)
    y = pt // 4
    cp = Copies(send, recv, (pt, anc, z))

    def step(i, d, n):
        return lax.rem(i + d + n, n)

    peers = [device_of(x, y, c, step(z, d, NZ)) for d in range(1, NZ)]
    peers += [device_of(step(x, d, NX), y, c, z) for d in range(1, NX)]
    peers += [device_of(x, step(y, d, NX), c, z) for d in range(1, NX)]
    sibling = device_of(x, y, 1 - c, z)
    peers += [sibling]
    barrier = pltpu.get_barrier_semaphore()
    for peer in peers:
        pl.semaphore_signal(barrier, inc=1, device_id=peer, device_id_type=MESH)

    pairs = (
        (points.at[pl.ds(0, H)], gp.at[0, z]), (points.at[pl.ds(H, H)], gp.at[1, z]), (idx_in, idx), (gain_in, gain),
        (wkv, vkv), (wqs, vqs), (wqv, vqv),
        (wo.at[pl.ds(0, W // 2)], wall.at[z, 0]), (wo.at[pl.ds(W // 2, W // 2)], wall.at[z, 1]),
    )
    loads = [pltpu.make_async_copy(src, dst, wsem.at[i]) for i, (src, dst) in enumerate(pairs)]
    for load in loads:
        load.start()
    loads[0].wait()
    loads[1].wait()
    pl.semaphore_wait(barrier, len(peers))

    def z_up(d):
        return device_of(x, y, c, step(z, d, NZ))


    def z_gather(at, rows):
        ids = [cp.new() for _ in range(8)]
        first, second = pl.ds(0, rows // 2), pl.ds(rows // 2, rows // 2)

        def begin():
            for k, d in enumerate((2, -2, 1, -1)):
                cp.start(ids[k], at(z), at(z), z_up(d))

        def forward():
            here = at(step(z, -2, NZ))
            cp.wait(ids[0], here)
            cp.start(ids[4], here, here, z_up(1))
            cp.start(ids[6], here.at[first], here.at[first], z_up(2))
            here = at(step(z, 2, NZ))
            cp.wait(ids[1], here)
            cp.start(ids[5], here, here, z_up(-1))
            cp.start(ids[7], here.at[second], here.at[second], z_up(-2))

        def near():
            cp.wait(ids[2], at(step(z, -1, NZ)))
            cp.wait(ids[3], at(step(z, 1, NZ)))

        def end():
            cp.wait(ids[4], at(step(z, -3, NZ)))
            cp.wait(ids[5], at(step(z, 3, NZ)))
            here = at(step(z, 4, NZ))
            cp.wait(ids[6], here.at[first])
            cp.wait(ids[7], here.at[second])

        return begin, forward, near, end

    halves = [z_gather(lambda i, e=e: gp.at[e, i], H) for e in range(2)]
    for begin, _, _, _ in halves:
        begin()

    def tally(first, count):
        total = jnp.zeros((64, LANES), F32)
        for i in range(count):
            row = idx[:, pl.ds((first + i) * 1024, 1024)]
            upper = (row // 128 == lax.broadcasted_iota(jnp.int32, (64, 1024), 0)).astype(F32)
            lower = (lax.rem(row, 128) == lax.broadcasted_iota(jnp.int32, (128, 1024), 0)).astype(F32)
            total = total + nt(upper.astype(BF16), lower.astype(BF16))
        return total

    loads[2].wait()
    surface = tally(0, 4)
    volume = tally(4, 4)
    everyone = surface + volume
    open_all = branch[0] == 1

    def log_count(n):
        return jnp.where(n > 0.0, jnp.log(jnp.maximum(n, 1.0)), NEG)

    for t, n in enumerate((jnp.where(open_all, everyone, volume), everyone)):
        rest = log_count(n)
        for j in range(3):
            term = rest.astype(BF16).astype(F32)
            logs[3 * t + j] = term
            rest = rest - term
    for _, forward, _, _ in halves:
        forward()

    u, v = (1 - c) * x + c * y, (1 - c) * y + c * x

    def place(i, j):
        return (1 - c) * i + c * j, (1 - c) * j + c * i

    def group_at(slot):
        du, dv = ORDER[slot % 16]
        if slot < 16:
            bx, by = place(step(u, du, NX), step(v, dv, NX))
            return group_of(bx, by, c)
        bx, by = place(step(u, dv, NX), step(v, du, NX))
        return group_of(bx, by, 1 - c)

    sub = lax.broadcasted_iota(jnp.int32, (8, LANES), 0)
    for slot in range(G):
        g = group_at(slot)
        for half in range(2):
            terms = jnp.zeros((8, LANES), F32)
            for j in range(6):
                terms = jnp.where(sub == j, logs[j, pl.ds(2 * g + half, 1)], terms)
            terms = jnp.concatenate([terms, jnp.zeros((LANES - 8, LANES), F32)], axis=0)
            ext[slot, pl.ds(half * LANES, LANES)] = jnp.transpose(terms).astype(BF16)

    for load in loads[3:]:
        load.wait()

    def project_half(e):
        total = jnp.zeros((H, LANES), F32)
        for i in range(NZ):
            part = gp[e, i].astype(F32)
            total = total + part * part
        scale = lax.rsqrt(jnp.sum(total, axis=-1, keepdims=True) * (1.0 / D) + 1e-06)
        for i in range(NZ):
            columns = pl.ds(i * W, W)
            nrm[e, :, columns] = (gp[e, i].astype(F32) * scale * gain[:, columns]).astype(BF16)
        kv[0, e, W : 2 * W] = dot(nrm[e], vkv[0]).astype(BF16)
        kv[0, e, 0:W] = jnp.transpose(dot(nrm[e], vkv[1])).astype(BF16)

    def toward(du, dv):
        bx, by = place(step(u, du, NX), step(v, dv, NX))
        return device_of(bx, by, c, z)

    u_ids = [[cp.new() for _ in range(3)] for _ in range(2)]
    v_ids = [[[cp.new() for _ in range(3)] for _ in range(4)] for _ in range(2)]
    s_ids = [cp.new() for _ in range(16)]

    def pass_on(k, e, src, dst, device):
        cp.start(k, kv.at[SLOT[src], e], kv.at[SLOT[dst], e], device)

    def landed(k, e, pair):
        cp.wait(k, kv.at[SLOT[pair], e])

    def share(e, du):
        pass_on(v_ids[e][du][0], e, (du, 0), (du, 3), toward(0, 1))
        pass_on(v_ids[e][du][1], e, (du, 0), (du, 1), toward(0, -1))

    def across(*pairs):
        for pair in pairs:
            slot = SLOT[pair]
            cp.start(s_ids[slot], kv.at[slot], kv.at[16 + slot], sibling)

    def from_sibling(first, count):
        for slot in range(first, first + count):
            cp.wait(s_ids[slot], kv.at[16 + slot])

    def kv_begin(e):
        pass_on(u_ids[e][0], e, (0, 0), (3, 0), toward(1, 0))
        pass_on(u_ids[e][1], e, (0, 0), (1, 0), toward(-1, 0))
        share(e, 0)
        pass_on(u_ids[e][2], e, (0, 0), (2, 0), toward(2, 0))

    def u_hop(e):
        for k, du in ((0, 3), (1, 1), (2, 2)):
            landed(u_ids[e][k], e, (du, 0))
            share(e, du)

    def v_hop(e, du):
        landed(v_ids[e][du][e], e, (du, 3 - 2 * e))
        pass_on(v_ids[e][du][2], e, (du, 3 - 2 * e), (du, 2), toward(0, 1 - 2 * e))

    def v_rest(du):
        landed(v_ids[1][du][0], 1, (du, 3))
        landed(v_ids[0][du][1], 0, (du, 1))
        across((du, 3), (du, 1))

    def v_end(du):
        landed(v_ids[0][du][2], 0, (du, 2))
        landed(v_ids[1][du][2], 1, (du, 2))
        across((du, 2))

    halves[0][2]()
    halves[0][3]()
    project_half(0)
    kv_begin(0)
    halves[1][2]()
    halves[1][3]()
    w_begin, w_forward, w_near, w_end = z_gather(lambda i: wall.at[i, c], W // 2)
    w_ids = [cp.new() for _ in range(NZ)]

    def w_across(*distances):
        for d in distances:
            at = step(z, d, NZ)
            cp.start(w_ids[d], wall.at[at, c], wall.at[at, c], sibling)

    def w_wait():
        for d in range(1, NZ):
            cp.wait(w_ids[d], wall.at[step(z, d, NZ), 1 - c])

    w_begin()
    project_half(1)
    kv_begin(1)
    rows = nrm[...].reshape(T, D)
    qsv[0] = dot(rows, vqs[...]).astype(BF16) * BF16(0.125)
    qsv[1] = dot(rows, vqv[...]).astype(BF16) * BF16(0.125)

    mine = y // 2
    q_ids = [cp.new() for _ in range(4)]
    for d in (1, 2, 3):
        there = step(y, d, NX)
        cp.start(q_ids[d], qsv.at[there // 2], qa.at[c, y], device_of(x, there, c, z))
    qa[c, y] = qsv[mine]
    across((0, 0))

    lane = lax.broadcasted_iota(jnp.int32, (T, W), 1)

    def split_heads(t, rows):
        marks = jnp.where(lane // 3 == t, 1.0, 0.0).astype(BF16)
        for h in range(2):
            qe[t, h, :, 0:W] = jnp.where(lane // 64 == h, rows, 0.0).astype(BF16)
            qe[t, h, :, W : 2 * W] = marks

    split_heads(0, jnp.where(open_all, qsv[0].astype(F32), qsv[1].astype(F32)))
    stat[...] = jnp.full(stat.shape, 2.0 * NEG, F32)
    acc[...] = jnp.zeros(acc.shape, F32)
    ones = jnp.ones((16, T), BF16)

    def fill(t, h, first, buf):
        top = None
        for j in range(CHUNK):
            slot = first + j
            k = jnp.concatenate([kv[slot, e, W : 2 * W] for e in range(2)], axis=0)
            s = nt(jnp.concatenate([k, ext[slot]], axis=1), qe[t, h])
            buf[j] = s
            top = s if top is None else jnp.maximum(top, s)
        return jnp.max(top, axis=0, keepdims=True)

    def absorb(t, h, first, buf, top):
        old = stat[t, h, 0:1]
        new = jnp.maximum(old, top)
        factor = jnp.exp(old - new)
        stat[t, h, 0:1] = new
        added = None
        for j in range(CHUNK):
            p = jnp.exp(buf[j] - new).astype(BF16)
            values = jnp.concatenate([kv[first + j, e, pl.ds(h * 64, 64)] for e in range(2)], axis=1)
            values = jnp.concatenate([values, ones], axis=0)
            term = dot(values, p)
            added = term if added is None else added + term
        acc[t, h] = acc[t, h] * factor + added

    def attend(t, first, chunks):
        last = first + (chunks - 1) * CHUNK
        top = fill(t, 0, first, even)

        def one(i, top):
            at = first + i * CHUNK
            other = fill(t, 1, at, odd)
            absorb(t, 0, at, even, top)
            top = fill(t, 0, jnp.minimum(at + CHUNK, last), even)
            absorb(t, 1, at, odd, other)
            return top

        if chunks > 1:
            top = lax.fori_loop(0, chunks - 1, one, top)
        other = fill(t, 1, last, odd)
        absorb(t, 0, last, even, top)
        absorb(t, 1, last, odd, other)

    m_ids = [cp.new() for _ in range(NZ)]
    o_ids = [cp.new() for _ in range(NZ)]
    outward = (4, 3, 5, 2, 6, 1, 7)

    def part(i):
        return pl.ds(pl.multiple_of(i * PART, PART), PART)

    def finish(t):
        parts = [acc[t, h, 0:64] / acc[t, h, 64:65] for h in range(2)]
        mixed[t] = jnp.transpose(jnp.concatenate(parts, axis=0)).astype(BF16)

    def exchange():
        for d in outward:
            cp.start(m_ids[d], mixed.at[:, part(step(z, d, NZ))], rows_in.at[z], z_up(d))
        rows_in[z] = mixed[:, part(z)]

    def project():
        for d in range(1, NZ):
            cp.wait(m_ids[d], rows_in.at[step(z, -d, NZ)])
        rows = jnp.concatenate([rows_in[i].reshape(2 * PART, W) for i in range(NZ)], axis=1)
        product = dot(rows, wall[...].reshape(D, D)).astype(BF16)
        for i in range(NZ):
            rows_out[i] = product[:, i * W : (i + 1) * W].reshape(2, PART, W)
        for d in outward:
            cp.start(o_ids[d], rows_out.at[step(z, d, NZ)], done.at[z], z_up(d))
        done[z] = rows_out[z]

    def write():
        for d in range(1, NZ):
            cp.wait(o_ids[d], done.at[step(z, -d, NZ)])
        for i in range(NZ):
            for t in range(2):
                out[t, i * PART : (i + 1) * PART] = done[i, t]

    x_ids = [cp.new() for _ in range(4)]

    def select():
        for d in (1, 2, 3, 0):
            there = step(x, d, NX)
            g = group_of(there, y, c)
            for half in range(2):
                named = idx[:, pl.ds(pl.multiple_of(g * T + half * LANES, LANES), LANES)]
                named = jnp.transpose(jnp.broadcast_to(named, (LANES, LANES)))
                named = jnp.concatenate([named, named], axis=1)
                found = jnp.zeros((LANES, W), F32)
                for core in range(2):
                    for row in range(NX):
                        base = group_of(x, row, core) * T
                        here = named - base == lax.broadcasted_iota(jnp.int32, (LANES, T), 1)
                        found = found + dot(here.astype(F32).astype(BF16), qa[core, row])
                rows = pl.ds(half * LANES, LANES)
                if d:
                    qstage[d - 1, rows] = found.astype(BF16)
                else:
                    qx[x, rows] = found.astype(BF16)
            if d:
                cp.start(x_ids[d], qstage.at[d - 1], qx.at[x], device_of(there, y, c, z))

    u_hop(0)
    v_hop(0, 0)
    u_hop(1)
    for d in (1, 2, 3):
        cp.wait(q_ids[d], qa.at[c, step(y, -d, NX)])
    cp.start(q_ids[0], qa.at[c], qa.at[c], sibling)
    v_hop(1, 0)
    across((3, 0), (1, 0), (2, 0))
    for du in (3, 1, 2):
        v_hop(0, du)
    attend(0, 0, 1)
    v_rest(0)
    for du in (3, 1, 2):
        v_hop(1, du)
    cp.wait(q_ids[0], qa.at[1 - c])
    select()
    w_forward()
    w_near()
    w_across(1, 2, 6, 7)
    for du in (3, 1, 2):
        v_rest(du)
    v_end(0)
    attend(0, 4, 2)
    for du in (3, 1, 2):
        v_end(du)
    for d in (1, 2, 3):
        cp.wait(x_ids[d], qx.at[step(x, -d, NX)])
    split_heads(1, sum(qx[i].astype(F32) for i in range(NX)))
    attend(1, 0, 3)
    attend(0, 12, 1)
    attend(1, 12, 1)
    from_sibling(0, 8)
    attend(0, 16, 2)
    attend(1, 16, 2)
    w_end()
    w_across(3, 4, 5)
    from_sibling(8, 4)
    attend(0, 24, 1)
    attend(1, 24, 1)
    from_sibling(12, 4)
    attend(0, 28, 1)
    attend(1, 28, 1)
    finish(0)
    finish(1)
    exchange()
    w_wait()
    cp.drain(len(cp.sent) - len(outward))
    project()
    cp.drain(len(outward))
    write()
    cp.drain(len(outward))


def shards(points, anchor_index, tile_branch, norm_gain, q_surface, q_volume, kv_weight, out_weight):
    vmem = pl.BlockSpec(memory_space=pltpu.VMEM)
    anywhere = pl.BlockSpec(memory_space=pl.ANY)
    smem = pl.BlockSpec(memory_space=pltpu.SMEM)
    both = pl.pallas_call(
        kernel,
        out_shape=jax.ShapeDtypeStruct((2, T, W), BF16),
        in_specs=[anywhere, anywhere, smem, anywhere, anywhere, anywhere, anywhere, anywhere],
        out_specs=vmem,
        scratch_shapes=[
            pltpu.VMEM((1, G * T), jnp.int32),
            pltpu.VMEM((1, D), F32),
            pltpu.VMEM((2, NZ, H, W), BF16),
            pltpu.VMEM((2, H, D), BF16),
            pltpu.VMEM((D, W), BF16),
            pltpu.VMEM((D, W), BF16),
            pltpu.VMEM((2, D, W), BF16),
            pltpu.VMEM((NZ, 2, W // 2, D), BF16),
            pltpu.VMEM((G, 2, 2 * W, H), BF16),
            pltpu.VMEM((G, T, LANES), BF16),
            pltpu.VMEM((8, 64, LANES), F32),
            pltpu.VMEM((2, T, W), BF16),
            pltpu.VMEM((2, NX, T, W), BF16),
            pltpu.VMEM((NX, T, W), BF16),
            pltpu.VMEM((3, T, W), BF16),
            pltpu.VMEM((2, 2, T, 2 * W), BF16),
            pltpu.VMEM((2, 2, 8, T), F32),
            pltpu.VMEM((2, 2, 80, T), F32),
            pltpu.VMEM((CHUNK, T, T), F32),
            pltpu.VMEM((CHUNK, T, T), F32),
            pltpu.VMEM((2, T, W), BF16),
            pltpu.VMEM((NZ, 2, PART, W), BF16),
            pltpu.VMEM((NZ, 2, PART, W), BF16),
            pltpu.VMEM((NZ, 2, PART, W), BF16),
            pltpu.SemaphoreType.DMA((9,)),
            pltpu.SemaphoreType.DMA((N_COPIES,)),
            pltpu.SemaphoreType.DMA((N_COPIES,)),
        ],
        compiler_params=pltpu.CompilerParams(
            collective_id=0, has_side_effects=True, vmem_limit_bytes=60 * 1024 * 1024
        ),
    )(
        points,
        anchor_index.reshape(1, -1),
        tile_branch,
        norm_gain.reshape(1, -1),
        q_surface,
        q_volume,
        kv_weight,
        out_weight,
    )
    return both[0], both[1]


def solution(mesh):
    in_specs = (
        P(("pt", "anc"), "head"),
        P(),
        P(("pt", "anc")),
        P(),
        P(None, "head"),
        P(None, "head"),
        P(None, None, "head"),
        P("head", None),
    )
    out_specs = (P(("pt", "anc"), "head"), P(("pt", "anc"), "head"))
    return jax.shard_map(shards, mesh=mesh, in_specs=in_specs, out_specs=out_specs, check_vma=False)
```

time: 70.1 us -> 63.1 us (0.900)
  Pallas kernels: 65.9 us -> 60.1 us
    pallas_call x1, Pallas kernels: 65.9 us -> 60.1 us  [shards(): pl.pallas_call(kernel, out_shape=jax.ShapeDtypeStruct((2, T, W), BF16), i...]
    unnamed x4 -> x0, local copies, waits for them, and re-layouts: 2.14 us -> none
    squeeze x0 -> x1, local copies, waits for them, and re-layouts: none -> 1.53 us  [shards(): return (both[0], both[1])]
where the time goes in v3:
time: 63.1 us; the launch traced here: 62.9 us
  Pallas kernels  60.1 us (95%)
  local copies, waits for them, and re-layouts  1.53 us (2%)
  between operations  1.29 us (2%)
    pallas_call x1, Pallas kernels, shards(): pl.pallas_call(kernel, out_shape=jax.ShapeDtypeStruct((2, T, W), BF16), i...  60.1 us
    squeeze x1, local copies, waits for them, and re-layouts, shards(): return (both[0], both[1])  1.53 us

profile of v3, /device:TPU:8, one launch (start us, length us, event | category | flops | bytes accessed | tf_op | source)
XLA Modules:
  0.0 62.9 jit_solution(1669616700736697059)
XLA Ops:
  1.3 60.1 %shard_map.95 = bf16[2,256,128]{2,1,0:T(8,128)(2,1)} custom-call(bf16[256,128]{1,0:T(8,128)(2,1)} %points.1, s32[1,8192]{1,0:T(1,128)} %bitcast.6, s32[1]{0:T(128)S(6)} %copy.10.branch, f32[1,1024]{1,0:T(1,128)} %bitcast.7, bf16[1024,128]{1,0:T(8,128)(2,1)} %wqs.1, bf16[1024,128]{1,0:T(8,128)(2,1)} %wqv.1, bf16[2,1024,128]{2,1,0:T(8,128)(2,1)} %wkv.1, ...), custom_call_target="tpu_custom_call" | custom-call | tf_op jit(solution)/shard_map/pallas_call | solution.py:476
  61.4 1.5 %slice_bitcast_fusion = (bf16[256,128]{1,0:T(8,128)(2,1)}, bf16[256,128]{1,0:T(8,128)(2,1)}) fusion(bf16[2,256,128]{2,1,0:T(8,128)(2,1)} %shard_map.95), kind=kLoop, calls=%fused_computation | loop fusion | bytes 262144 | tf_op jit(solution)/shard_map/squeeze | solution.py:523

commit v4 on v3

--- a/solution.py
+++ b/solution.py
@@ -270,10 +270,29 @@
         landed(v_ids[1][du][2], 1, (du, 2))
         across((du, 2))
 
+    mine = y // 2
+    q_ids = [[cp.new() for _ in range(4)] for _ in range(2)]
+
+    def queries(e):
+        rows = pl.ds(e * H, H)
+        qsv[0, rows] = dot(nrm[e], vqs[...]).astype(BF16) * BF16(0.125)
+        qsv[1, rows] = dot(nrm[e], vqv[...]).astype(BF16) * BF16(0.125)
+        for d in (1, 2, 3):
+            there = step(y, d, NX)
+            cp.start(q_ids[e][d], qsv.at[there // 2, rows], qa.at[c, y, rows], device_of(x, there, c, z))
+        qa[c, y, rows] = qsv[mine, rows]
+
+    def q_across():
+        for e in range(2):
+            for d in (1, 2, 3):
+                cp.wait(q_ids[e][d], qa.at[c, step(y, -d, NX), pl.ds(e * H, H)])
+        cp.start(q_ids[0][0], qa.at[c], qa.at[c], sibling)
+
     halves[0][2]()
     halves[0][3]()
     project_half(0)
     kv_begin(0)
+    queries(0)
     halves[1][2]()
     halves[1][3]()
     w_begin, w_forward, w_near, w_end = z_gather(lambda i: wall.at[i, c], W // 2)
@@ -291,16 +310,7 @@
     w_begin()
     project_half(1)
     kv_begin(1)
-    rows = nrm[...].reshape(T, D)
-    qsv[0] = dot(rows, vqs[...]).astype(BF16) * BF16(0.125)
-    qsv[1] = dot(rows, vqv[...]).astype(BF16) * BF16(0.125)
-
-    mine = y // 2
-    q_ids = [cp.new() for _ in range(4)]
-    for d in (1, 2, 3):
-        there = step(y, d, NX)
-        cp.start(q_ids[d], qsv.at[there // 2], qa.at[c, y], device_of(x, there, c, z))
-    qa[c, y] = qsv[mine]
+    queries(1)
     across((0, 0))
 
     lane = lax.broadcasted_iota(jnp.int32, (T, W), 1)
@@ -357,6 +367,16 @@
         other = fill(t, 1, last, odd)
         absorb(t, 0, last, even, top)
         absorb(t, 1, last, odd, other)
+
+    def attend_both(first):
+        top = fill(0, 0, first, even)
+        other = fill(0, 1, first, odd)
+        absorb(0, 0, first, even, top)
+        top = fill(1, 0, first, even)
+        absorb(0, 1, first, odd, other)
+        other = fill(1, 1, first, odd)
+        absorb(1, 0, first, even, top)
+        absorb(1, 1, first, odd, other)
 
     m_ids = [cp.new() for _ in range(NZ)]
     o_ids = [cp.new() for _ in range(NZ)]
@@ -419,9 +439,7 @@
     u_hop(0)
     v_hop(0, 0)
     u_hop(1)
-    for d in (1, 2, 3):
-        cp.wait(q_ids[d], qa.at[c, step(y, -d, NX)])
-    cp.start(q_ids[0], qa.at[c], qa.at[c], sibling)
+    q_across()
     v_hop(1, 0)
     across((3, 0), (1, 0), (2, 0))
     for du in (3, 1, 2):
@@ -430,34 +448,34 @@
     v_rest(0)
     for du in (3, 1, 2):
         v_hop(1, du)
-    cp.wait(q_ids[0], qa.at[1 - c])
+    cp.wait(q_ids[0][0], qa.at[1 - c])
     select()
-    w_forward()
-    w_near()
-    w_across(1, 2, 6, 7)
     for du in (3, 1, 2):
         v_rest(du)
     v_end(0)
     attend(0, 4, 2)
     for du in (3, 1, 2):
         v_end(du)
+    from_sibling(0, 8)
+    w_forward()
+    w_near()
+    w_across(1, 2, 6, 7)
+    attend(0, 12, 3)
     for d in (1, 2, 3):
         cp.wait(x_ids[d], qx.at[step(x, -d, NX)])
     split_heads(1, sum(qx[i].astype(F32) for i in range(NX)))
-    attend(1, 0, 3)
-    attend(0, 12, 1)
-    attend(1, 12, 1)
-    from_sibling(0, 8)
-    attend(0, 16, 2)
-    attend(1, 16, 2)
+    attend(1, 0, 6)
+
+    def last(i, carry):
+        for k in range(CHUNK):
+            slot = 8 + i * CHUNK + k
+            cp.wait(s_ids[0] + slot, kv.at[16 + slot])
+        attend_both(24 + i * CHUNK)
+        return carry
+
+    lax.fori_loop(0, 2, last, 0)
     w_end()
     w_across(3, 4, 5)
-    from_sibling(8, 4)
-    attend(0, 24, 1)
-    attend(1, 24, 1)
-    from_sibling(12, 4)
-    attend(0, 28, 1)
-    attend(1, 28, 1)
     finish(0)
     finish(1)
     exchange()

time: 63.1 us -> 61.2 us (0.970)
  Pallas kernels: 60.1 us -> 58.2 us
    pallas_call x1, Pallas kernels: 60.1 us -> 58.2 us  [shards(): pl.pallas_call(kernel, out_shape=jax.ShapeDtypeStruct((2, T, W), BF16), i...]
where the time goes in v4:
time: 61.2 us; the launch traced here: 61 us
  Pallas kernels  58.2 us (95%)
  local copies, waits for them, and re-layouts  1.53 us (2%)
  between operations  1.29 us (2%)
    pallas_call x1, Pallas kernels, shards(): pl.pallas_call(kernel, out_shape=jax.ShapeDtypeStruct((2, T, W), BF16), i...  58.2 us
    squeeze x1, local copies, waits for them, and re-layouts, shards(): return (both[0], both[1])  1.53 us

profile of v4, /device:TPU:8, one launch (start us, length us, event | category | flops | bytes accessed | tf_op | source)
XLA Modules:
  0.0 61.0 jit_solution(11063217159804330364)
XLA Ops:
  1.3 58.2 %shard_map.95 = bf16[2,256,128]{2,1,0:T(8,128)(2,1)} custom-call(bf16[256,128]{1,0:T(8,128)(2,1)} %points.1, s32[1,8192]{1,0:T(1,128)} %bitcast.6, s32[1]{0:T(128)S(6)} %copy.10.branch, f32[1,1024]{1,0:T(1,128)} %bitcast.7, bf16[1024,128]{1,0:T(8,128)(2,1)} %wqs.1, bf16[1024,128]{1,0:T(8,128)(2,1)} %wqv.1, bf16[2,1024,128]{2,1,0:T(8,128)(2,1)} %wkv.1, ...), custom_call_target="tpu_custom_call" | custom-call | tf_op jit(solution)/shard_map/pallas_call | solution.py:494
  59.5 1.5 %slice_bitcast_fusion = (bf16[256,128]{1,0:T(8,128)(2,1)}, bf16[256,128]{1,0:T(8,128)(2,1)}) fusion(bf16[2,256,128]{2,1,0:T(8,128)(2,1)} %shard_map.95), kind=kLoop, calls=%fused_computation | loop fusion | bytes 262144 | tf_op jit(solution)/shard_map/squeeze | solution.py:541

commit v5 on v4

--- a/solution.py
+++ b/solution.py
@@ -98,10 +98,6 @@
     peers += [device_of(x, step(y, d, NX), c, z) for d in range(1, NX)]
     sibling = device_of(x, y, 1 - c, z)
     peers += [sibling]
-    barrier = pltpu.get_barrier_semaphore()
-    for peer in peers:
-        pl.semaphore_signal(barrier, inc=1, device_id=peer, device_id_type=MESH)
-
     pairs = (
         (points.at[pl.ds(0, H)], gp.at[0, z]), (points.at[pl.ds(H, H)], gp.at[1, z]), (idx_in, idx), (gain_in, gain),
         (wkv, vkv), (wqs, vqs), (wqv, vqv),
@@ -110,6 +106,10 @@
     loads = [pltpu.make_async_copy(src, dst, wsem.at[i]) for i, (src, dst) in enumerate(pairs)]
     for load in loads:
         load.start()
+    barrier = pltpu.get_barrier_semaphore()
+    for peer in peers:
+        pl.semaphore_signal(barrier, inc=1, device_id=peer, device_id_type=MESH)
+
     loads[0].wait()
     loads[1].wait()
     pl.semaphore_wait(barrier, len(peers))
@@ -474,11 +474,11 @@
         return carry
 
     lax.fori_loop(0, 2, last, 0)
-    w_end()
-    w_across(3, 4, 5)
     finish(0)
     finish(1)
     exchange()
+    w_end()
+    w_across(3, 4, 5)
     w_wait()
     cp.drain(len(cp.sent) - len(outward))
     project()

time: 61.2 us -> 61.1 us (level)
  no operation moved by 1% of the time
where the time goes in v5:
time: 61.1 us; the launch traced here: 61 us
  Pallas kernels  58.2 us (95%)
  local copies, waits for them, and re-layouts  1.53 us (3%)
  between operations  1.29 us (2%)
    pallas_call x1, Pallas kernels, shards(): pl.pallas_call(kernel, out_shape=jax.ShapeDtypeStruct((2, T, W), BF16), i...  58.2 us
    squeeze x1, local copies, waits for them, and re-layouts, shards(): return (both[0], both[1])  1.53 us

profile of v5, /device:TPU:8, one launch (start us, length us, event | category | flops | bytes accessed | tf_op | source)
XLA Modules:
  0.0 61.0 jit_solution(9129309930549049510)
XLA Ops:
  1.3 58.2 %shard_map.95 = bf16[2,256,128]{2,1,0:T(8,128)(2,1)} custom-call(bf16[256,128]{1,0:T(8,128)(2,1)} %points.1, s32[1,8192]{1,0:T(1,128)} %bitcast.6, s32[1]{0:T(128)S(6)} %copy.10.branch, f32[1,1024]{1,0:T(1,128)} %bitcast.7, bf16[1024,128]{1,0:T(8,128)(2,1)} %wqs.1, bf16[1024,128]{1,0:T(8,128)(2,1)} %wqv.1, bf16[2,1024,128]{2,1,0:T(8,128)(2,1)} %wkv.1, ...), custom_call_target="tpu_custom_call" | custom-call | tf_op jit(solution)/shard_map/pallas_call | solution.py:494
  59.5 1.5 %slice_bitcast_fusion = (bf16[256,128]{1,0:T(8,128)(2,1)}, bf16[256,128]{1,0:T(8,128)(2,1)}) fusion(bf16[2,256,128]{2,1,0:T(8,128)(2,1)} %shard_map.95), kind=kLoop, calls=%fused_computation | loop fusion | bytes 262144 | tf_op jit(solution)/shard_map/squeeze | solution.py:541
